TPU v7x, 512 devices: a whole 4x8x8 slice. The times are simulated.
512 devices in a mesh: section: 8 (over z), expert: 64 (over x, y, core).
Axes of the slice: x: 4, y: 8, z: 8, core: 2. Of those that a mesh axis runs over, the one named last changes fastest.
Arguments:
- held: bfloat16 [8, 256, 5120], P('section', 'expert'), may hold values from -6 to 6
- arrivals: bfloat16 [3, 256, 5120], P(None, 'expert'), may hold values from -6 to 6
- expert_ids: int32 [4, 8, 256, 1], P(None, 'section', 'expert'), may hold values from 0 to 1; in each aligned block of 4 rows (0 to 3, 4 to 7, ..., all dimensions but the last counted through in order) at most 3 rows name the same one
- router_scores: float32 [4, 8, 256], P(None, 'section', 'expert'), may hold values from -6 to 6
- norm_gain: float32 [8, 5120], P('section'), may hold values from 0.25 to 1.75
- w_gate: bfloat16 [8, 5120, 8192], P('section', None, 'expert'), may hold values from -0.078125 to 0.078125
- w_up: bfloat16 [8, 5120, 8192], P('section', None, 'expert'), may hold values from -0.078125 to 0.078125
- w_down: bfloat16 [8, 8192, 5120], P('section', 'expert'), may hold values from -0.09375 to 0.09375
Outputs:
- section_out: bfloat16 [4, 8, 256, 5120], P(None, 'section', 'expert')
Inputs may be any that keep to these rules, and one draw needn't show every extreme that they name: `expert_ids`: within the rows of one device (aligned blocks of 4 rows of the flattened leading dimensions) no expert is named by more than 3 rows, a bound that some block reaches.
All inputs are finite; a program needn't handle non-finite values.
Results may differ from a plain program's by a relative error of at most 0.009.
Values may be sent and summed in bfloat16 or wider, within the bound.
A program may use at most 64 MiB of HBM per device.

v0:
```python
import jax
import jax.numpy as jnp
from jax import lax
from jax.sharding import PartitionSpec as P

FLIGHT = 2
STEPS = 4
CAP = 3


def passed_along(value, axis, steps):
    count = lax.axis_size(axis)
    initial, last = (max(0, -steps), min(count, count - steps))
    return lax.ppermute(value, axis, [(source, source + steps) for source in range(initial, last)])


def normalize(values, gain):
    wide = values.astype(jnp.float32)
    power = jnp.mean(wide * wide, axis=-1, keepdims=True)
    return (wide * lax.rsqrt(power + 1e-05) * gain).astype(jnp.bfloat16)


def per_device(held, arrivals, expert_ids, router_scores, norm_gain, w_gate, w_up, w_down):
    experts = lax.axis_size("expert")
    group_size = experts // FLIGHT
    section_num = lax.axis_index("section")
    width = held.shape[2]
    gate_w = w_gate[0]
    up_w = w_up[0]
    down_w = w_down[0]
    gain = norm_gain[0]
    incoming = held[0]
    collected = []
    for step in range(STEPS):
        if step > 0:
            current = jnp.where(section_num == 0, arrivals[step - 1], incoming)
        else:
            current = incoming
        chosen = expert_ids[step, 0, :, 0]
        normed = normalize(current, gain)
        match = (chosen[:, None] == jnp.arange(FLIGHT, dtype=jnp.int32)[None, :]).astype(jnp.int32)
        before = jnp.cumsum(match, axis=0) - match
        slot_num = jnp.sum(before * match, axis=1)
        position = chosen * CAP + slot_num
        select = (jnp.arange(FLIGHT * CAP, dtype=jnp.int32)[:, None] == position[None, :]).astype(
            jnp.bfloat16
        )
        per_expert = jnp.dot(select, normed, preferred_element_type=jnp.float32).astype(
            jnp.bfloat16
        )
        per_expert = per_expert.reshape(FLIGHT, CAP, width)
        outgoing = jnp.repeat(per_expert, group_size, axis=0)
        arrived = lax.all_to_all(outgoing, "expert", split_axis=0, concat_axis=0, tiled=True)
        flat = arrived.reshape(-1, width)
        gate_out = jnp.dot(flat, gate_w, preferred_element_type=jnp.float32)
        up_out = jnp.dot(flat, up_w, preferred_element_type=jnp.float32)
        hidden = (jax.nn.silu(gate_out) * up_out).astype(jnp.bfloat16)
        result = jnp.dot(hidden, down_w, preferred_element_type=jnp.float32).astype(jnp.bfloat16)
        returned = lax.all_to_all(
            result.reshape(arrived.shape), "expert", split_axis=0, concat_axis=0, tiled=True
        )
        summed = jnp.sum(
            returned.astype(jnp.float32).reshape(FLIGHT, group_size, CAP, width), axis=1
        )
        picked = lax.dot_general(
            select.astype(jnp.float32),
            summed.reshape(-1, width),
            (((0,), (0,)), ((), ())),
            precision=lax.Precision.HIGHEST,
            preferred_element_type=jnp.float32,
        )
        weight = jax.nn.sigmoid(router_scores[step, 0])
        result = (current.astype(jnp.float32) + weight[:, None] * picked).astype(jnp.bfloat16)
        collected.append(result)
        if step + 1 < STEPS:
            incoming = passed_along(result, "section", 1)
    return jnp.stack(collected)[:, None]


def solution(mesh):
    placed = (
        P("section", "expert", None),
        P(None, "expert", None),
        P(None, "section", "expert", None),
        P(None, "section", "expert"),
        P("section", None),
        P("section", None, "expert"),
        P("section", None, "expert"),
        P("section", "expert", None),
    )
    return jax.shard_map(
        per_device,
        mesh=mesh,
        in_specs=placed,
        out_specs=P(None, "section", "expert", None),
        check_vma=False,
    )
```

profile of v0, /device:TPU:199, one launch (start us, length us, event | category | flops | bytes accessed | tf_op | source)
XLA Modules:
  0.0 653.4 jit_solution(6237547907396314537)
XLA Ops:
  5.0 73.1 %all_to_all.40 = bf16[64,3,5120]{2,1,0:T(4,128)(2,1)} all-to-all(bf16[64,3,5120]{2,1,0:T(4,128)(2,1)S(1)} %bitcast.130), channel_id=1, replica_groups=mesh['section'=8,'expert'=64] {'expert'}, dimensions={0} | all-to-all | bytes 3932160 | tf_op jit(solution)/shard_map/all_to_all | solution.py:53
  78.1 4.7 reshape.212
  85.1 4.5 convolution_convert_fusion.3
  89.6 4.3 reshape.213
  93.9 6.7 %all-to-all-start.1 = ((bf16[64,3,5120]{2,1,0:T(4,128)(2,1)}), bf16[64,3,5120]{2,1,0:T(4,128)(2,1)}, u32[]{:S(2)}, u32[]{:S(2)}) async-start(bf16[64,3,5120]{2,1,0:T(4,128)(2,1)} %reshape.213), calls=%async_computation.1 | async-start | bytes 5242880 | tf_op jit(solution)/shard_map/all_to_all | solution.py:59
  100.7 62.0 %all-to-all-done.1 = bf16[64,3,5120]{2,1,0:T(4,128)(2,1)} async-done(((bf16[64,3,5120]{2,1,0:T(4,128)(2,1)}), bf16[64,3,5120]{2,1,0:T(4,128)(2,1)}, u32[]{:S(2)}, u32[]{:S(2)}) %all-to-all-start.1) | async-done | bytes 1966112 | tf_op jit(solution)/shard_map/all_to_all | solution.py:59
  165.9 5.2 collective-permute-start
  173.3 68.9 %all_to_all.41 = bf16[64,3,5120]{2,1,0:T(4,128)(2,1)} all-to-all(bf16[64,3,5120]{2,1,0:T(4,128)(2,1)S(1)} %bitcast.131), channel_id=1, replica_groups=mesh['section'=8,'expert'=64] {'expert'}, dimensions={0} | all-to-all | bytes 3932160 | tf_op jit(solution)/shard_map/all_to_all | solution.py:53
  242.2 4.6 reshape.219
  249.0 4.5 convolution_convert_fusion.2
  253.5 4.3 reshape.220
  257.8 68.7 %all_to_all.42 = bf16[64,3,5120]{2,1,0:T(4,128)(2,1)S(1)} all-to-all(bf16[64,3,5120]{2,1,0:T(4,128)(2,1)} %reshape.220), channel_id=1, replica_groups=mesh['section'=8,'expert'=64] {'expert'}, dimensions={0} | all-to-all | bytes 3932160 | tf_op jit(solution)/shard_map/all_to_all | solution.py:59
  328.0 5.2 collective-permute-start.1
  335.4 69.3 %all_to_all.43 = bf16[64,3,5120]{2,1,0:T(4,128)(2,1)} all-to-all(bf16[64,3,5120]{2,1,0:T(4,128)(2,1)S(1)} %bitcast.132), channel_id=1, replica_groups=mesh['section'=8,'expert'=64] {'expert'}, dimensions={0} | all-to-all | bytes 3932160 | tf_op jit(solution)/shard_map/all_to_all | solution.py:53
  404.7 4.6 reshape.226
  411.5 4.5 convolution_convert_fusion.1
  416.0 4.3 reshape.227
  420.3 68.5 %all_to_all.44 = bf16[64,3,5120]{2,1,0:T(4,128)(2,1)S(1)} all-to-all(bf16[64,3,5120]{2,1,0:T(4,128)(2,1)} %reshape.227), channel_id=1, replica_groups=mesh['section'=8,'expert'=64] {'expert'}, dimensions={0} | all-to-all | bytes 3932160 | tf_op jit(solution)/shard_map/all_to_all | solution.py:59
  490.2 5.2 collective-permute-start.2
  497.6 69.3 %all_to_all.45 = bf16[64,3,5120]{2,1,0:T(4,128)(2,1)} all-to-all(bf16[64,3,5120]{2,1,0:T(4,128)(2,1)S(1)} %bitcast.133), channel_id=1, replica_groups=mesh['section'=8,'expert'=64] {'expert'}, dimensions={0} | all-to-all | bytes 3932160 | tf_op jit(solution)/shard_map/all_to_all | solution.py:53
  566.9 4.6 reshape.233
  573.8 4.5 convolution_convert_fusion
  578.3 4.3 reshape.234
  582.6 68.5 %all_to_all.46 = bf16[64,3,5120]{2,1,0:T(4,128)(2,1)S(1)} all-to-all(bf16[64,3,5120]{2,1,0:T(4,128)(2,1)} %reshape.234), channel_id=1, replica_groups=mesh['section'=8,'expert'=64] {'expert'}, dimensions={0} | all-to-all | bytes 3932160 | tf_op jit(solution)/shard_map/all_to_all | solution.py:59
  (65 shorter events, 28.5 us)
Async XLA Ops:
  0.0 85.1 %copy-start = (bf16[1,128,5120]{2,1,0:T(8,128)(2,1)S(1)}, bf16[1,128,5120]{2,1,0:T(8,128)(2,1)}, u32[]{:S(2)}) copy-start(bf16[1,128,5120]{2,1,0:T(8,128)(2,1)} %param.15) | copy-start | bytes 3932164
  78.1 4.7 copy-start.1
  93.9 6.7 %copy-start.4 = (f32[4,1,4]{2,1,0:T(1,128)S(1)}, f32[4,1,4]{2,1,0:T(1,128)}, u32[]{:S(2)}) copy-start(f32[4,1,4]{2,1,0:T(1,128)} %param.11) | copy-start | bytes 196
  93.9 68.8 %all-to-all-start.1 = ((bf16[64,3,5120]{2,1,0:T(4,128)(2,1)}), bf16[64,3,5120]{2,1,0:T(4,128)(2,1)}, u32[]{:S(2)}, u32[]{:S(2)}) async-start(bf16[64,3,5120]{2,1,0:T(4,128)(2,1)} %reshape.213), calls=%async_computation.1 | async-start | bytes 5242880 | tf_op jit(solution)/shard_map/all_to_all | solution.py:59
  100.7 64.9 %copy-start.2 = (bf16[1,4,5120]{2,1,0:T(4,128)(2,1)S(1)}, bf16[1,4,5120]{2,1,0:T(4,128)(2,1)}, u32[]{:S(2)}) copy-start(bf16[1,4,5120]{2,1,0:T(4,128)(2,1)} %param.8) | copy-start | bytes 122884
  100.7 71.5 %copy-start.3 = (bf16[3,4,5120]{2,1,0:T(4,128)(2,1)S(1)}, bf16[3,4,5120]{2,1,0:T(4,128)(2,1)}, u32[]{:S(2)}) copy-start(bf16[3,4,5120]{2,1,0:T(4,128)(2,1)} %param.9) | copy-start | bytes 368644
  100.7 71.7 %copy-start.5 = (f32[1,5120]{1,0:T(1,128)S(1)}, f32[1,5120]{1,0:T(1,128)}, u32[]{:S(2)}) copy-start(f32[1,5120]{1,0:T(1,128)} %param.12) | copy-start | bytes 61444
  165.9 6.3 collective-permute-start
  328.0 6.3 collective-permute-start.1
  490.2 6.3 collective-permute-start.2
where the time goes:
time: 655 us; the launch traced here: 653 us
  blocking collectives  486 us (74%)
  waiting for transfers between devices  65.2 us (10%)
  local copies, waits for them, and re-layouts  39.9 us (6%)
  matrix products  29.5 us (5%)
  starting transfers between devices  22.3 us (3%)
  other arithmetic  9.79 us (1%)
    all_to_all x4, blocking collectives, per_device(): lax.all_to_all(outgoing, 'expert', split_axis=0, concat_axis=0, tiled=True)  281 us
    all_to_all x3, blocking collectives, per_device(): lax.all_to_all(result.reshape(arrived.shape), 'expert', split_axis=0, con...  206 us
    all_to_all x1, waiting for transfers between devices, per_device(): lax.all_to_all(result.reshape(arrived.shape), 'expert', split_axis=0, con...  62 us
    reshape x4, local copies, waits for them, and re-layouts, per_device(): flat = arrived.reshape(-1, width)  18.6 us
    dot_general x4, matrix products, per_device(): jnp.dot(hidden, down_w, preferred_element_type=jnp.float32)  17.9 us
    reshape x4, local copies, waits for them, and re-layouts, per_device(): result.reshape(arrived.shape)  17.4 us
    ppermute x3, starting transfers between devices, passed_along(): lax.ppermute(value, axis, [(source, source + steps) for source in range(i...  15.5 us
  transfers between devices with their start and end apart: 4, of which 4 were waited for; matrix products, arithmetic and copies ran while one was open for 0% of the time, Pallas kernels for 0%

commit v1 on v0

v1 whole, which is shorter than its diff:
```python
import functools

import jax
import jax.numpy as jnp
from jax import lax
from jax.experimental import pallas as pl
from jax.experimental.pallas import tpu as pltpu
from jax.sharding import PartitionSpec as P

MESH = pl.DeviceIdType.MESH
T = 4
NX, NY = 4, 8
D = 5120
HALF = D // 2
Q = HALF // 4
UNITS = 128
DY = (0, 1, -1, 2, -2, 3, -3, 4)
INV = (0, 2, 1, 4, 3, 6, 5, 7)
BATCH = ((0, 1), (1, 2), (3, 2), (5, 3))
BATCH_OF = (0, 1, 1, 2, 2, 3, 3, 3)
F32, BF16 = jnp.float32, jnp.bfloat16


def kernel(
    rows_ref, gain_ref, ids_ref, score_ref, wg_ref, wu_ref, wd_ref, out_ref,
    wgu, wdn, perm, perm_t, cur, nb, zbuf, zsrc, ag, idb, mask, xs, part, exs, exr,
    rs, r1, fr, fs, ysrc, yr,
    w_send, w_recv, w_local, id_send, id_recv, idx_recv,
    s_own, s_x, s_x2, s_ex, s_rs, s_fs, s_y, s_z,
    r_ag, r_x, r_x2, r_ex, r_r1, r_pure, r_sum, r_y, r_yc, r_z,
):
    section = lax.axis_index("section")
    me = lax.axis_index("expert")
    core = me % 2
    py = (me // 2) % NY
    px = me // (2 * NY)

    def at(dx, dy, c):
        return {"expert": (((px + dx + NX) % NX) * NY + (py + dy + NY) % NY) * 2 + c}

    sibling = at(0, 0, 1 - core)

    def send(src, dst, send_sem, recv_sem, device):
        pltpu.make_async_remote_copy(
            src_ref=src, dst_ref=dst, send_sem=send_sem, recv_sem=recv_sem,
            device_id=device, device_id_type=MESH,
        ).start()

    def wait(ref, sem):
        pltpu.make_async_copy(ref, ref, sem).wait()

    mine = pl.multiple_of(core * HALF, HALF)
    other = pl.multiple_of((1 - core) * HALF, HALF)
    unit = pl.multiple_of(core * UNITS, UNITS)
    local = [
        pltpu.make_async_copy(
            wg_ref.at[pl.ds(mine, HALF)], wgu.at[0, :, pl.ds(unit, UNITS)], w_local.at[0]),
        pltpu.make_async_copy(
            wu_ref.at[pl.ds(mine, HALF)], wgu.at[1, :, pl.ds(unit, UNITS)], w_local.at[1]),
        pltpu.make_async_copy(
            wd_ref.at[:, pl.ds(mine, HALF)], wdn.at[pl.ds(unit, UNITS)], w_local.at[2]),
    ]
    for copy in local:
        copy.start()

    barrier = pltpu.get_barrier_semaphore()
    partners = [sibling]
    partners += [at(0, dy, c) for dy in DY[1:] for c in range(2)]
    partners += [at(dx, 0, c) for dx in (1, -1) for c in range(2)]
    partners += [{"section": (section + 1) % 8}, {"section": (section + 7) % 8}]
    for device in partners:
        pl.semaphore_signal(barrier, inc=1, device_id=device, device_id_type=MESH)

    i = lax.broadcasted_iota(jnp.int32, (256, 256), 0)
    j = lax.broadcasted_iota(jnp.int32, (256, 256), 1)
    perm[...] = jnp.where(
        (i // 64 == (j % 16) // 4) & ((i % 64) // 4 == j // 16) & (i % 4 == j % 4), 1.0, 0.0
    ).astype(BF16)
    perm_t[...] = jnp.where(
        (j // 64 == (i % 16) // 4) & ((j % 64) // 4 == i // 16) & (i % 4 == j % 4), 1.0, 0.0
    ).astype(BF16)
    for a in range(2):
        @pl.when(core == a)
        def _():
            idb[a, 0, 0] = ids_ref[...]

    pl.semaphore_wait(barrier, len(partners))

    remote = [
        (wg_ref.at[pl.ds(other, HALF)], wgu.at[0, :, pl.ds(unit, UNITS)]),
        (wu_ref.at[pl.ds(other, HALF)], wgu.at[1, :, pl.ds(unit, UNITS)]),
        (wd_ref.at[:, pl.ds(other, HALF)], wdn.at[pl.ds(unit, UNITS)]),
    ]

    def spread(t, a):
        @pl.when(core == a)
        def _():
            @pl.when((t > 0) & (section > 0))
            def _():
                wait(zbuf.at[t], r_z.at[t])
                cur[...] = zbuf[t].astype(F32)

            @pl.when((t == 0) | (section == 0))
            def _():
                cur[...] = rows_ref[t].astype(F32)

            wide = cur[...]
            power = jnp.broadcast_to(jnp.sum(wide * wide, axis=1, keepdims=True), (32, 128))
            for shift in (4, 8, 16):
                power = power + pltpu.roll(power, shift, 0)
            scale = lax.rsqrt(power[:, :1] * (1.0 / D) + 1e-05)
            normed = (wide * scale * gain_ref[...]).astype(BF16)
            nb[t, 0] = normed[:16]
            nb[t, 1] = normed[16:]
            for slot in range(1, 8):
                for h in range(2):
                    send(nb.at[t, h], ag.at[t, a, 0, INV[slot]], s_own.at[t, 0],
                         r_ag.at[t, a, BATCH_OF[INV[slot]]], at(0, DY[slot], h))
            for h in range(2):
                send(nb.at[t, h], ag.at[t, a, 1, 0], s_own.at[t, 1], r_x.at[t, a, 0, 0], at(1, 0, h))
                send(nb.at[t, h], ag.at[t, a, 2, 0], s_own.at[t, 1], r_x.at[t, a, 1, 0], at(-1, 0, h))
            send(nb.at[t, 1 - core], ag.at[t, a, 0, 0], s_own.at[t, 1], r_ag.at[t, a, 0], sibling)
            ag[t, a, 0, 0] = nb[t, core]

    def along_y(t, a, k):
        first, count = BATCH[k]
        block = ag.at[t, a, 0, pl.ds(first, count)]
        wait(block, r_ag.at[t, a, k])
        send(block, ag.at[t, a, 1, pl.ds(first, count)], s_x.at[t, a, 0], r_x.at[t, a, 0, k], at(1, 0, core))
        send(block, ag.at[t, a, 2, pl.ds(first, count)], s_x.at[t, a, 1], r_x.at[t, a, 1, k], at(-1, 0, core))

    def along_x(t, a, k):
        first, count = BATCH[k]
        low = ag.at[t, a, 1, pl.ds(first, count)]
        high = ag.at[t, a, 2, pl.ds(first, count)]
        wait(low, r_x.at[t, a, 0, k])
        wait(high, r_x.at[t, a, 1, k])
        dst = ag.at[t, a, 3, pl.ds(first, count)]
        if k in (0, 3):
            send(low, dst, s_x2.at[t, a], r_x2.at[t, a], at(1, 0, core))
        else:
            send(high, dst, s_x2.at[t, a], r_x2.at[t, a], at(-1, 0, core))

    def gate_up(t, a):
        wait(ag.at[t, a, 3], r_x2.at[t, a])

        @pl.when(core != a)
        def _():
            wait(ag.at[t, a, 0, 0], r_ag.at[t, a, 0])

        for g in range(2):
            block = ag[t, a, 2 * g:2 * g + 2].reshape(256, Q)
            moved = jnp.dot(perm[...], block, preferred_element_type=F32).astype(BF16)
            for q in range(4):
                xs[a, 64 * g:64 * g + 64, Q * q:Q * q + Q] = moved[64 * q:64 * q + 64]
        for w in range(2):
            value = jnp.dot(xs[a], wgu[w], preferred_element_type=F32)
            part[a, :, 256 * w:256 * w + 256] = value
            exs[t, a, :, 256 * w:256 * w + 256] = value.astype(BF16)
        send(exs.at[t, a], exr.at[t, a], s_ex.at[t, a], r_ex.at[t, a], sibling)

    def down(t, a):
        wait(exr.at[t, a], r_ex.at[t, a])
        gate = part[a, :, :256] + exr[t, a, :, :256].astype(F32)
        up = part[a, :, 256:] + exr[t, a, :, 256:].astype(F32)
        keep = mask[t, a]
        hidden = (gate / (1.0 + jnp.exp(-gate)) * up * jnp.concatenate([keep, keep], axis=1)).astype(BF16)
        result = jnp.dot(hidden, wdn[...], preferred_element_type=F32).astype(BF16)
        for g in (1, 0):
            piece = jnp.concatenate(
                [result[64 * g:64 * g + 64, Q * q:Q * q + Q] for q in range(4)], axis=0)
            moved = jnp.dot(perm_t[...], piece, preferred_element_type=F32).astype(BF16)
            rs[t, a, 2 * g:2 * g + 2] = moved.reshape(2, 8, 16, Q)
            if g == 1:
                send(rs.at[t, a, 3, pl.ds(0, 4)], r1.at[t, a, 0], s_rs.at[t, a, 0], r_r1.at[t, a, 0], at(1, 0, core))
                send(rs.at[t, a, 3, pl.ds(4, 4)], r1.at[t, a, 1], s_rs.at[t, a, 1], r_r1.at[t, a, 1], at(-1, 0, core))
                send(rs.at[t, a, 2, pl.ds(4, 4)], fr.at[t, a, 0, pl.ds(4, 4)], s_rs.at[t, a, 2], r_pure.at[t, a, 0],
                     at(1, 0, core))
            else:
                send(rs.at[t, a, 1, pl.ds(0, 4)], fr.at[t, a, 1, pl.ds(0, 4)], s_rs.at[t, a, 3], r_pure.at[t, a, 1],
                     at(-1, 0, core))

    def back_x(t, a):
        wait(r1.at[t, a, 0], r_r1.at[t, a, 0])
        fs[t, a, 0] = (rs[t, a, 2, 0:4].astype(F32) + r1[t, a, 0].astype(F32)).astype(BF16)
        send(fs.at[t, a, 0], fr.at[t, a, 0, pl.ds(0, 4)], s_fs.at[t, a, 0], r_sum.at[t, a, 0], at(1, 0, core))
        wait(r1.at[t, a, 1], r_r1.at[t, a, 1])
        fs[t, a, 1] = (rs[t, a, 1, 4:8].astype(F32) + r1[t, a, 1].astype(F32)).astype(BF16)
        send(fs.at[t, a, 1], fr.at[t, a, 1, pl.ds(4, 4)], s_fs.at[t, a, 1], r_sum.at[t, a, 1], at(-1, 0, core))

    def back_y(t, a):
        wait(fr.at[t, a, 0, pl.ds(4, 4)], r_pure.at[t, a, 0])
        wait(fr.at[t, a, 1, pl.ds(0, 4)], r_pure.at[t, a, 1])
        wait(fr.at[t, a, 0, pl.ds(0, 4)], r_sum.at[t, a, 0])
        wait(fr.at[t, a, 1, pl.ds(4, 4)], r_sum.at[t, a, 1])
        for slot in (7, 6, 5, 4, 3, 2, 1, 0):
            ysrc[t, a, slot] = (
                rs[t, a, 0, slot].astype(F32) + fr[t, a, 0, slot].astype(F32) + fr[t, a, 1, slot].astype(F32)
            ).astype(BF16)
            if slot:
                send(ysrc.at[t, a, slot], yr.at[t, core, INV[slot]], s_y.at[t, a, 0], r_y.at[t], at(0, DY[slot], a))

        @pl.when(core == a)
        def _():
            yr[t, core, 0] = ysrc[t, a, 0]

        @pl.when(core != a)
        def _():
            send(ysrc.at[t, a, 0], yr.at[t, core, 0], s_y.at[t, a, 1], r_yc.at[t], sibling)

    def finish(t, a):
        @pl.when(core == a)
        def _():
            wait(yr.at[t, 1 - core, 0], r_yc.at[t])
            wait(yr.at[t, :, pl.ds(1, 7)], r_y.at[t])
            weight = 1.0 / (1.0 + jnp.exp(-score_ref[t]))
            for h in range(2):
                total = yr[t, h, 0].astype(F32)
                for slot in range(1, 8):
                    total = total + yr[t, h, slot].astype(F32)
                value = cur[16 * h:16 * h + 16] + weight[16 * h:16 * h + 16, :1] * total
                zsrc[t, 16 * h:16 * h + 16] = value.astype(BF16)

            @pl.when((t < T - 1) & (section < 7))
            def _():
                send(zsrc.at[t], zbuf.at[t + 1], s_z.at[t], r_z.at[t + 1], {"section": (section + 1) % 8})

            out_ref[t] = zsrc[t]

    def masks():
        for a in range(2):
            wait(idb.at[a, 0, pl.ds(1, 7)], id_recv.at[a, 0])

            @pl.when(core != a)
            def _():
                wait(idb.at[a, 0, 0], id_recv.at[a, 1])

            send(idb.at[a, 0], idb.at[a, 1], id_send.at[2 + 3 * a], idx_recv.at[a, 0], at(1, 0, core))
            send(idb.at[a, 0], idb.at[a, 2], id_send.at[3 + 3 * a], idx_recv.at[a, 1], at(-1, 0, core))
        for a in range(2):
            wait(idb.at[a, 1], idx_recv.at[a, 0])
            wait(idb.at[a, 2], idx_recv.at[a, 1])
            send(idb.at[a, 1], idb.at[a, 3], id_send.at[4 + 3 * a], idx_recv.at[a, 2], at(1, 0, core))

    def masks_end():
        expert = (px // (NX // 2)).astype(F32)
        for a in range(2):
            wait(idb.at[a, 3], idx_recv.at[a, 2])
            for g in range(2):
                named = jnp.dot(
                    perm[...], idb[a, 2 * g:2 * g + 2].reshape(256, 128), preferred_element_type=F32)
                for t in range(T):
                    mask[t, a, 64 * g:64 * g + 64] = jnp.where(named[64 * t:64 * t + 64] == expert, 1.0, 0.0)

    def tick(t, first):
        for a in range(2):
            spread(t, a)
        if first:
            for k, (src, dst) in enumerate(remote):
                send(src, dst, w_send.at[k], w_recv.at[k], sibling)
            for a in range(2):
                @pl.when(core == a)
                def _():
                    for slot in range(1, 8):
                        for h in range(2):
                            send(ids_ref, idb.at[a, 0, INV[slot]], id_send.at[0], id_recv.at[a, 0], at(0, DY[slot], h))
                    send(ids_ref, idb.at[a, 0, 0], id_send.at[1], id_recv.at[a, 1], sibling)
        for k in (1, 0, 2, 3):
            for a in range(2):
                if k:
                    along_y(t, a, k)
                else:
                    along_x(t, a, 0)
        if first:
            masks()
        for k in (1, 2, 3):
            for a in range(2):
                along_x(t, a, k)
        if first:
            masks_end()
            for copy in local:
                copy.wait()
            for k, (_, dst) in enumerate(remote):
                wait(dst, w_recv.at[k])
        for stage in (gate_up, down, back_x, back_y, finish):
            for a in range(2):
                stage(t, a)

    tick(0, True)

    def later(t, _):
        tick(t, False)
        return 0

    lax.fori_loop(1, T, later, 0)

    for k, (src, _) in enumerate(remote):
        wait(src, w_send.at[k])
    wait(idb.at[:, 0, pl.ds(0, 7)], id_send.at[0])
    wait(ids_ref, id_send.at[1])
    for a in range(2):
        for k in range(3):
            wait(idb.at[a, k], id_send.at[2 + 3 * a + k])

    def drain(t, _):
        wait(yr.at[t, :, pl.ds(1, 7)], s_own.at[t, 0])
        wait(yr.at[t, 0, pl.ds(0, 5)], s_own.at[t, 1])
        for a in range(2):
            for d in range(2):
                wait(ag.at[t, a, 0, pl.ds(1, 7)], s_x.at[t, a, d])
                wait(fs.at[t, a, d], s_fs.at[t, a, d])
            wait(ag.at[t, a, 3], s_x2.at[t, a])
            wait(exs.at[t, a], s_ex.at[t, a])
            for k in range(4):
                wait(rs.at[t, a, k, pl.ds(0, 4)], s_rs.at[t, a, k])
            wait(ysrc.at[t, a, pl.ds(1, 7)], s_y.at[t, a, 0])

            @pl.when(core != a)
            def _():
                wait(ysrc.at[t, a, 0], s_y.at[t, a, 1])

        @pl.when((t < T - 1) & (section < 7))
        def _():
            wait(zsrc.at[t], s_z.at[t])
        return 0

    lax.fori_loop(0, T, drain, 0)


def per_device(held, arrivals, expert_ids, router_scores, norm_gain, w_gate, w_up, w_down):
    rows = jnp.concatenate([held, arrivals], axis=0).reshape(T, 4, 8, Q)
    rows = rows.transpose(0, 2, 1, 3).reshape(T, 32, Q)
    gain = jnp.repeat(norm_gain[0].reshape(8, Q), 4, axis=0)
    ids = jnp.broadcast_to(expert_ids.reshape(16, 1).astype(BF16), (16, 128))
    scores = jnp.broadcast_to(jnp.tile(router_scores[:, 0], (1, 8))[:, :, None], (T, 32, 128))
    vmem, anywhere = pl.BlockSpec(memory_space=pltpu.VMEM), pl.BlockSpec(memory_space=pl.ANY)
    dma = pltpu.SemaphoreType.DMA
    out = pl.pallas_call(
        kernel,
        out_shape=jax.ShapeDtypeStruct((T, 32, Q), BF16),
        in_specs=[vmem] * 4 + [anywhere] * 3,
        out_specs=vmem,
        scratch_shapes=[
            pltpu.VMEM((2, HALF, 256), BF16),
            pltpu.VMEM((256, HALF), BF16),
            pltpu.VMEM((256, 256), BF16),
            pltpu.VMEM((256, 256), BF16),
            pltpu.VMEM((32, Q), F32),
            pltpu.VMEM((T, 2, 16, Q), BF16),
            pltpu.VMEM((T, 32, Q), BF16),
            pltpu.VMEM((T, 32, Q), BF16),
            pltpu.VMEM((T, 2, 4, 8, 16, Q), BF16),
            pltpu.VMEM((2, 4, 8, 16, 128), BF16),
            pltpu.VMEM((T, 2, 128, 128), F32),
            pltpu.VMEM((2, 128, HALF), BF16),
            pltpu.VMEM((2, 128, 512), F32),
            pltpu.VMEM((T, 2, 128, 512), BF16),
            pltpu.VMEM((T, 2, 128, 512), BF16),
            pltpu.VMEM((T, 2, 4, 8, 16, Q), BF16),
            pltpu.VMEM((T, 2, 2, 4, 16, Q), BF16),
            pltpu.VMEM((T, 2, 2, 8, 16, Q), BF16),
            pltpu.VMEM((T, 2, 2, 4, 16, Q), BF16),
            pltpu.VMEM((T, 2, 8, 16, Q), BF16),
            pltpu.VMEM((T, 2, 8, 16, Q), BF16),
            dma((3,)), dma((3,)), dma((3,)), dma((8,)), dma((2, 2)), dma((2, 3)),
            dma((T, 2)), dma((T, 2, 2)), dma((T, 2)), dma((T, 2)), dma((T, 2, 4)), dma((T, 2, 2)),
            dma((T, 2, 2)), dma((T,)),
            dma((T, 2, 4)), dma((T, 2, 2, 4)), dma((T, 2)), dma((T, 2)), dma((T, 2, 2)), dma((T, 2, 2)),
            dma((T, 2, 2)), dma((T,)), dma((T,)), dma((T,)),
        ],
        compiler_params=pltpu.CompilerParams(
            collective_id=0, has_side_effects=True, vmem_limit_bytes=56 << 20
        ),
        name="relay",
    )(rows, gain, ids, scores, w_gate[0], w_up[0], w_down[0])
    out = out.reshape(T, 8, 4, Q).transpose(0, 2, 1, 3).reshape(T, 1, 4, D)
    return out


def solution(mesh):
    placed = (
        P("section", "expert", None),
        P(None, "expert", None),
        P(None, "section", "expert", None),
        P(None, "section", "expert"),
        P("section", None),
        P("section", None, "expert"),
        P("section", None, "expert"),
        P("section", "expert", None),
    )
    return jax.shard_map(
        per_device,
        mesh=mesh,
        in_specs=placed,
        out_specs=P(None, "section", "expert", None),
        check_vma=False,
    )
```

time: 655 us -> 197 us (0.30)
  the two profiles are of different devices: /device:TPU:199 before, /device:TPU:193 now
where the time goes in v1:
time: 197 us
  Pallas kernels  188 us (95%)
  local copies, waits for them, and re-layouts  5.75 us (3%)
  other arithmetic  3.14 us (2%)
    pallas_call x1, Pallas kernels, per_device(): pl.pallas_call(kernel, out_shape=jax.ShapeDtypeStruct((T, 32, Q), BF16),...  188 us

profile of v1, /device:TPU:193, one launch (start us, length us, event | category | flops | bytes accessed | tf_op | source)
XLA Modules:
  0.0 196.9 jit_solution(11710198937029678293)
XLA Ops:
  0.0 0.7 convert_reduce_fusion
  0.7 0.1 convert_element_type.12
  0.8 0.7 broadcast_in_dim.14.ids_ref
  1.5 0.7 tile.10
  2.1 0.1 tile.11
  2.2 0.5 broadcast.8
  2.7 1.4 reduce.5
  4.2 0.7 reshape.32.gain_ref
  4.9 0.7 broadcast_in_dim.15.score_ref
  5.6 1.0 pad_maximum_fusion
  6.6 0.7 reshape.31.rows_ref
  7.3 188.0 %relay.1 = bf16[4,32,640]{2,1,0:T(8,128)(2,1)} custom-call(bf16[4,32,640]{2,1,0:T(8,128)(2,1)} %reshape.31.rows_ref, f32[32,640]{1,0:T(8,128)} %reshape.32.gain_ref, bf16[16,128]{1,0:T(8,128)(2,1)} %broadcast_in_dim.14.ids_ref, f32[4,32,128]{2,1,0:T(8,128)} %broadcast_in_dim.15.score_ref, bf16[5120,128]{1,0:T(8,128)(2,1)} %bitcast.10, ...), custom_call_target="tpu_custom_call" | custom-call | tf_op jit(solution)/shard_map/relay/pallas_call | solution.py:338
  195.3 1.6 reshape.33
  (2 shorter events, 0.0 us)

commit v2 on v1

v2 whole, which is shorter than its diff:
```python
import functools

import jax
import jax.numpy as jnp
from jax import lax
from jax.experimental import pallas as pl
from jax.experimental.pallas import tpu as pltpu
from jax.sharding import PartitionSpec as P

MESH = pl.DeviceIdType.MESH
T = 4
NX, NY = 4, 8
D = 5120
HALF = D // 2
Q = HALF // 4
UNITS = 128
DY = (0, 1, -1, 2, -2, 3, -3, 4)
INV = (0, 2, 1, 4, 3, 6, 5, 7)
BATCH = ((0, 1), (1, 2), (3, 2), (5, 3))
BATCH_OF = (0, 1, 1, 2, 2, 3, 3, 3)
ORDER = (
    "Asp", "Bd0'", "Bd1'", "Ay1", "Ax0", "Ay2", "Brf'", "Brn'", "Ay3", "Ax1", "Ax2", "Bbf'", "Bbn'", "Ax3",
    "Ag0", "Ag1", "Bfi'", "Bsp", "Ad0", "Ad1", "By1", "Bx0", "By2", "Arf", "Arn", "By3", "Bx1", "Bx2", "Abf",
    "Abn", "Bx3", "Bg0", "Bg1", "Afi",
)
F32, BF16 = jnp.float32, jnp.bfloat16


def kernel(
    held_ref, arrivals_ref, gain_in, ids_in, score_in, wg_ref, wu_ref, wd_ref, out_ref,
    gain_ref, ids_f, ids_ref, score_ref, wgu, wdn, perm, perm_t, cur, nb, zbuf, zsrc, ag, idb, mask, part, exs, exr,
    rs, r1, fr, fs, ysrc, yr,
    w_send, w_recv, w_local, id_send, id_recv, idx_recv,
    s_own, s_x, s_x2, s_ex, s_rs, s_fs, s_y, s_z,
    r_ag, r_x, r_x2, r_ex, r_r1, r_pure, r_sum, r_y, r_yc, r_z,
):
    section = lax.axis_index("section")
    me = lax.axis_index("expert")
    core = me % 2
    py = (me // 2) % NY
    px = me // (2 * NY)

    def at(dx, dy, c):
        return {"expert": (((px + dx + NX) % NX) * NY + (py + dy + NY) % NY) * 2 + c}

    sibling = at(0, 0, 1 - core)

    def send(src, dst, send_sem, recv_sem, device):
        pltpu.make_async_remote_copy(
            src_ref=src, dst_ref=dst, send_sem=send_sem, recv_sem=recv_sem,
            device_id=device, device_id_type=MESH,
        ).start()

    def wait(ref, sem):
        pltpu.make_async_copy(ref, ref, sem).wait()

    mine = pl.multiple_of(core * HALF, HALF)
    other = pl.multiple_of((1 - core) * HALF, HALF)
    unit = pl.multiple_of(core * UNITS, UNITS)
    local = [
        pltpu.make_async_copy(
            wg_ref.at[pl.ds(mine, HALF)], wgu.at[0, :, pl.ds(unit, UNITS)], w_local.at[0]),
        pltpu.make_async_copy(
            wu_ref.at[pl.ds(mine, HALF)], wgu.at[1, :, pl.ds(unit, UNITS)], w_local.at[1]),
        pltpu.make_async_copy(
            wd_ref.at[:, pl.ds(mine, HALF)], wdn.at[pl.ds(unit, UNITS)], w_local.at[2]),
    ]
    for copy in local:
        copy.start()

    barrier = pltpu.get_barrier_semaphore()
    partners = [sibling]
    partners += [at(0, dy, c) for dy in DY[1:] for c in range(2)]
    partners += [at(dx, 0, c) for dx in (1, -1) for c in range(2)] + [at(2, 0, core)]
    partners += [{"section": (section + 1) % 8}, {"section": (section + 7) % 8}]
    for device in partners:
        pl.semaphore_signal(barrier, inc=1, device_id=device, device_id_type=MESH)

    for k in range(8):
        gain_ref[4 * k:4 * k + 4] = jnp.broadcast_to(gain_in[:, Q * k:Q * k + Q], (4, Q))
    for t in range(T):
        for r in range(4):
            ids_f[4 * t + r:4 * t + r + 1] = jnp.broadcast_to(ids_in[t:t + 1, r:r + 1].astype(F32), (1, 128))
            weight = jnp.broadcast_to(1.0 / (1.0 + jnp.exp(-score_in[t:t + 1, r:r + 1])), (1, 128))
            for k in range(8):
                score_ref[t, 4 * k + r:4 * k + r + 1] = weight
    ids_ref[...] = ids_f[...].astype(BF16)

    i = lax.broadcasted_iota(jnp.int32, (256, 256), 0)
    j = lax.broadcasted_iota(jnp.int32, (256, 256), 1)
    perm[...] = jnp.where(
        (i // 64 == (j % 16) // 4) & ((i % 64) // 4 == j // 16) & (i % 4 == j % 4), 1.0, 0.0
    ).astype(BF16)
    perm_t[...] = jnp.where(
        (j // 64 == (i % 16) // 4) & ((j % 64) // 4 == i // 16) & (i % 4 == j % 4), 1.0, 0.0
    ).astype(BF16)
    for a in range(2):
        @pl.when(core == a)
        def _():
            idb[a, 0, 0] = ids_ref[...]

    pl.semaphore_wait(barrier, len(partners))

    remote = [
        (wg_ref.at[pl.ds(other, HALF)], wgu.at[0, :, pl.ds(unit, UNITS)]),
        (wu_ref.at[pl.ds(other, HALF)], wgu.at[1, :, pl.ds(unit, UNITS)]),
        (wd_ref.at[:, pl.ds(other, HALF)], wdn.at[pl.ds(unit, UNITS)]),
    ]

    def place(rows):
        for k in range(8):
            cur[4 * k:4 * k + 4] = rows[:, Q * k:Q * k + Q]

    def spread(t, a):
        @pl.when(core == a)
        def _():
            if not isinstance(t, int):
                @pl.when(section > 0)
                def _():
                    wait(zbuf.at[t], r_z.at[t])
                    cur[...] = zbuf[t].astype(F32)

            if isinstance(t, int):
                place(held_ref[...].astype(F32))
            else:
                @pl.when(section == 0)
                def _():
                    place(arrivals_ref[t - 1].astype(F32))

            wide = cur[...]
            power = jnp.broadcast_to(jnp.sum(wide * wide, axis=1, keepdims=True), (32, 128))
            for shift in (4, 8, 16):
                power = power + pltpu.roll(power, shift, 0)
            scale = lax.rsqrt(power[:, :1] * (1.0 / D) + 1e-05)
            normed = (wide * scale * gain_ref[...]).astype(BF16)
            nb[t, 0] = normed[:16]
            nb[t, 1] = normed[16:]
            for slot in (1, 2):
                for h in range(2):
                    send(nb.at[t, h], ag.at[t, a, 0, INV[slot]], s_own.at[t, 0],
                         r_ag.at[t, a, BATCH_OF[INV[slot]]], at(0, DY[slot], h))
            for h in range(2):
                send(nb.at[t, h], ag.at[t, a, 1, 0], s_own.at[t, 1], r_x.at[t, a, 0, 0], at(1, 0, h))
                send(nb.at[t, h], ag.at[t, a, 2, 0], s_own.at[t, 1], r_x.at[t, a, 1, 0], at(-1, 0, h))
            for slot in range(3, 8):
                for h in range(2):
                    send(nb.at[t, h], ag.at[t, a, 0, INV[slot]], s_own.at[t, 0],
                         r_ag.at[t, a, BATCH_OF[INV[slot]]], at(0, DY[slot], h))
            send(nb.at[t, 1 - core], ag.at[t, a, 0, 0], s_own.at[t, 1], r_ag.at[t, a, 0], sibling)
            ag[t, a, 0, 0] = nb[t, core]

    def along_y(t, a, k):
        first, count = BATCH[k]
        block = ag.at[t, a, 0, pl.ds(first, count)]
        wait(block, r_ag.at[t, a, k])
        send(block, ag.at[t, a, 1, pl.ds(first, count)], s_x.at[t, a, 0], r_x.at[t, a, 0, k], at(1, 0, core))
        send(block, ag.at[t, a, 2, pl.ds(first, count)], s_x.at[t, a, 1], r_x.at[t, a, 1, k], at(-1, 0, core))
        if k == 3:
            send(block, ag.at[t, a, 3, pl.ds(first, count)], s_x2.at[t, a], r_x2.at[t, a], at(2, 0, core))

    def along_x(t, a, k):
        first, count = BATCH[k]
        low = ag.at[t, a, 1, pl.ds(first, count)]
        high = ag.at[t, a, 2, pl.ds(first, count)]
        wait(low, r_x.at[t, a, 0, k])
        wait(high, r_x.at[t, a, 1, k])
        dst = ag.at[t, a, 3, pl.ds(first, count)]
        if k == 0:
            send(low, dst, s_x2.at[t, a], r_x2.at[t, a], at(1, 0, core))
        elif k < 3:
            send(high, dst, s_x2.at[t, a], r_x2.at[t, a], at(-1, 0, core))

    def gate_up(t, a, s):
        if s == 0:
            @pl.when(core != a)
            def _():
                wait(ag.at[t, a, 0, 0], r_ag.at[t, a, 0])
        else:
            wait(ag.at[t, a, 3], r_x2.at[t, a])
        low = 64 * s
        block = ag[t, a, 2 * s:2 * s + 2].reshape(256, Q)
        moved = jnp.dot(perm[...], block, preferred_element_type=F32).astype(BF16)
        rows = jnp.concatenate([moved[64 * q:64 * q + 64] for q in range(4)], axis=1)
        for w in range(2):
            value = jnp.dot(rows, wgu[w], preferred_element_type=F32)
            part[a, low:low + 64, 256 * w:256 * w + 256] = value
            exs[t, a, low:low + 64, 256 * w:256 * w + 256] = value.astype(BF16)
        mine_now = pl.ds(low, 64)
        send(exs.at[t, a, mine_now], exr.at[t, a, mine_now], s_ex.at[t, a, s], r_ex.at[t, a, s], sibling)

    def down(t, a, s):
        low = 64 * s
        wait(exr.at[t, a, pl.ds(low, 64)], r_ex.at[t, a, s])
        sums = part[a, low:low + 64] + exr[t, a, low:low + 64].astype(F32)
        gate, up = sums[:, :256], sums[:, 256:]
        keep = mask[t, a, low:low + 64]
        hidden = (gate / (1.0 + jnp.exp(-gate)) * up * jnp.concatenate([keep, keep], axis=1)).astype(BF16)
        result = jnp.dot(hidden, wdn[...], preferred_element_type=F32).astype(BF16)
        piece = jnp.concatenate([result[:, Q * q:Q * q + Q] for q in range(4)], axis=0)
        moved = jnp.dot(perm_t[...], piece, preferred_element_type=F32).astype(BF16)
        rs[t, a, 2 * s:2 * s + 2] = moved.reshape(2, 8, 16, Q)
        near, far = pl.ds(0, 4), pl.ds(4, 4)
        if s:
            send(rs.at[t, a, 3, far], r1.at[t, a, 1], s_rs.at[t, a, 1], r_r1.at[t, a, 1], at(-1, 0, core))
            send(rs.at[t, a, 3, near], r1.at[t, a, 0], s_rs.at[t, a, 0], r_r1.at[t, a, 0], at(1, 0, core))
            send(rs.at[t, a, 2, far], fr.at[t, a, 0, far], s_rs.at[t, a, 2], r_pure.at[t, a, 0], at(1, 0, core))
        else:
            send(rs.at[t, a, 1, near], fr.at[t, a, 1, near], s_rs.at[t, a, 3], r_pure.at[t, a, 1], at(-1, 0, core))

    def relay(t, a, far):
        low = 4 * far
        here, step = (1, -1) if far else (2, 1)
        wait(r1.at[t, a, far], r_r1.at[t, a, far])
        fs[t, a, far] = (rs[t, a, here, low:low + 4].astype(F32) + r1[t, a, far].astype(F32)).astype(BF16)
        send(fs.at[t, a, far], fr.at[t, a, far, pl.ds(low, 4)], s_fs.at[t, a, far], r_sum.at[t, a, far],
             at(step, 0, core))

    def back_y(t, a, far):
        block = pl.ds(4 * far, 4)
        wait(fr.at[t, a, 1 - far, block], r_pure.at[t, a, 1 - far])
        wait(fr.at[t, a, far, block], r_sum.at[t, a, far])
        for slot in range(4 * far + 3, 4 * far - 1, -1):
            ysrc[t, a, slot] = (
                rs[t, a, 0, slot].astype(F32) + fr[t, a, 0, slot].astype(F32) + fr[t, a, 1, slot].astype(F32)
            ).astype(BF16)
            if slot:
                send(ysrc.at[t, a, slot], yr.at[t, core, INV[slot]], s_y.at[t, a, 0], r_y.at[t], at(0, DY[slot], a))
        if not far:
            @pl.when(core == a)
            def _():
                yr[t, core, 0] = ysrc[t, a, 0]

            @pl.when(core != a)
            def _():
                send(ysrc.at[t, a, 0], yr.at[t, core, 0], s_y.at[t, a, 1], r_yc.at[t], sibling)

    def finish(t, a):
        @pl.when(core == a)
        def _():
            wait(yr.at[t, 1 - core, 0], r_yc.at[t])
            wait(yr.at[t, :, pl.ds(1, 7)], r_y.at[t])
            weight = score_ref[t]
            for h in range(2):
                total = yr[t, h, 0].astype(F32)
                for slot in range(1, 8):
                    total = total + yr[t, h, slot].astype(F32)
                value = cur[16 * h:16 * h + 16] + weight[16 * h:16 * h + 16, :1] * total
                zsrc[t, 16 * h:16 * h + 16] = value.astype(BF16)
                for q in range(4):
                    k = 4 * h + q
                    out_ref[t, :, Q * k:Q * k + Q] = value[4 * q:4 * q + 4].astype(BF16)

            @pl.when((t < T - 1) & (section < 7))
            def _():
                send(zsrc.at[t], zbuf.at[t + 1], s_z.at[t], r_z.at[t + 1], {"section": (section + 1) % 8})

    def masks():
        for a in range(2):
            wait(idb.at[a, 0, pl.ds(1, 7)], id_recv.at[a, 0])

            @pl.when(core != a)
            def _():
                wait(idb.at[a, 0, 0], id_recv.at[a, 1])

            send(idb.at[a, 0], idb.at[a, 1], id_send.at[2 + 3 * a], idx_recv.at[a, 0], at(1, 0, core))
            send(idb.at[a, 0], idb.at[a, 2], id_send.at[3 + 3 * a], idx_recv.at[a, 1], at(-1, 0, core))
        for a in range(2):
            wait(idb.at[a, 1], idx_recv.at[a, 0])
            wait(idb.at[a, 2], idx_recv.at[a, 1])
            send(idb.at[a, 1], idb.at[a, 3], id_send.at[4 + 3 * a], idx_recv.at[a, 2], at(1, 0, core))

    def masks_end():
        expert = (px // (NX // 2)).astype(F32)
        for a in range(2):
            wait(idb.at[a, 3], idx_recv.at[a, 2])
            for g in range(2):
                named = jnp.dot(
                    perm[...], idb[a, 2 * g:2 * g + 2].reshape(256, 128), preferred_element_type=F32)
                for t in range(T):
                    mask[t, a, 64 * g:64 * g + 64] = jnp.where(named[64 * t:64 * t + 64] == expert, 1.0, 0.0)

    def start():
        for k, (src, dst) in enumerate(remote):
            send(src, dst, w_send.at[k], w_recv.at[k], sibling)
        for a in range(2):
            @pl.when(core == a)
            def _():
                for slot in range(1, 8):
                    for h in range(2):
                        send(ids_ref, idb.at[a, 0, INV[slot]], id_send.at[0], id_recv.at[a, 0], at(0, DY[slot], h))
                send(ids_ref, idb.at[a, 0, 0], id_send.at[1], id_recv.at[a, 1], sibling)

    def ready():
        masks()
        masks_end()
        for copy in local:
            copy.wait()
        for k, (_, dst) in enumerate(remote):
            wait(dst, w_recv.at[k])

    stages = {
        "sp": spread, "fi": finish,
        "y1": lambda t, a: along_y(t, a, 1), "y2": lambda t, a: along_y(t, a, 2), "y3": lambda t, a: along_y(t, a, 3),
        "x0": lambda t, a: along_x(t, a, 0), "x1": lambda t, a: along_x(t, a, 1),
        "x2": lambda t, a: along_x(t, a, 2), "x3": lambda t, a: along_x(t, a, 3),
        "g0": lambda t, a: gate_up(t, a, 0), "g1": lambda t, a: gate_up(t, a, 1),
        "d0": lambda t, a: down(t, a, 0), "d1": lambda t, a: down(t, a, 1),
        "rf": lambda t, a: relay(t, a, 1), "rn": lambda t, a: relay(t, a, 0),
        "bf": lambda t, a: back_y(t, a, 1), "bn": lambda t, a: back_y(t, a, 0),
    }

    def tick(t, parts, first=False):
        for name in ORDER:
            late = name.endswith("'")
            if ("late" if late else "now") not in parts:
                continue
            if first and name == "Ag0":
                ready()
            stages[name[1:3]](t - 1 if late else t, "AB".index(name[0]))
            if first and name == "Asp":
                start()

    tick(0, ("now",), first=True)

    def later(t, _):
        tick(t, ("now", "late"))
        return 0

    lax.fori_loop(1, T, later, 0)
    tick(T, ("late",))

    for k, (src, _) in enumerate(remote):
        wait(src, w_send.at[k])
    wait(idb.at[:, 0, pl.ds(0, 7)], id_send.at[0])
    wait(ids_ref, id_send.at[1])
    for a in range(2):
        for k in range(3):
            wait(idb.at[a, k], id_send.at[2 + 3 * a + k])

    def drain(t, _):
        wait(yr.at[t, :, pl.ds(1, 7)], s_own.at[t, 0])
        wait(yr.at[t, 0, pl.ds(0, 5)], s_own.at[t, 1])
        for a in range(2):
            for d in range(2):
                wait(ag.at[t, a, 0, pl.ds(1, 7)], s_x.at[t, a, d])
                wait(fs.at[t, a, d], s_fs.at[t, a, d])
                wait(exs.at[t, a, pl.ds(64 * d, 64)], s_ex.at[t, a, d])
            wait(ag.at[t, a, 3], s_x2.at[t, a])
            for k in range(4):
                wait(rs.at[t, a, k, pl.ds(0, 4)], s_rs.at[t, a, k])
            wait(ysrc.at[t, a, pl.ds(1, 7)], s_y.at[t, a, 0])

            @pl.when(core != a)
            def _():
                wait(ysrc.at[t, a, 0], s_y.at[t, a, 1])

        @pl.when((t < T - 1) & (section < 7))
        def _():
            wait(zsrc.at[t], s_z.at[t])
        return 0

    lax.fori_loop(0, T, drain, 0)


def per_device(held, arrivals, expert_ids, router_scores, norm_gain, w_gate, w_up, w_down):
    vmem, anywhere = pl.BlockSpec(memory_space=pltpu.VMEM), pl.BlockSpec(memory_space=pl.ANY)
    dma = pltpu.SemaphoreType.DMA
    out = pl.pallas_call(
        kernel,
        out_shape=jax.ShapeDtypeStruct((T, 4, D), BF16),
        in_specs=[vmem] * 5 + [anywhere] * 3,
        out_specs=vmem,
        scratch_shapes=[
            pltpu.VMEM((32, Q), F32),
            pltpu.VMEM((16, 128), F32),
            pltpu.VMEM((16, 128), BF16),
            pltpu.VMEM((T, 32, 128), F32),
            pltpu.VMEM((2, HALF, 256), BF16),
            pltpu.VMEM((256, HALF), BF16),
            pltpu.VMEM((256, 256), BF16),
            pltpu.VMEM((256, 256), BF16),
            pltpu.VMEM((32, Q), F32),
            pltpu.VMEM((T, 2, 16, Q), BF16),
            pltpu.VMEM((T, 32, Q), BF16),
            pltpu.VMEM((T, 32, Q), BF16),
            pltpu.VMEM((T, 2, 4, 8, 16, Q), BF16),
            pltpu.VMEM((2, 4, 8, 16, 128), BF16),
            pltpu.VMEM((T, 2, 128, 128), F32),
            pltpu.VMEM((2, 128, 512), F32),
            pltpu.VMEM((T, 2, 128, 512), BF16),
            pltpu.VMEM((T, 2, 128, 512), BF16),
            pltpu.VMEM((T, 2, 4, 8, 16, Q), BF16),
            pltpu.VMEM((T, 2, 2, 4, 16, Q), BF16),
            pltpu.VMEM((T, 2, 2, 8, 16, Q), BF16),
            pltpu.VMEM((T, 2, 2, 4, 16, Q), BF16),
            pltpu.VMEM((T, 2, 8, 16, Q), BF16),
            pltpu.VMEM((T, 2, 8, 16, Q), BF16),
            dma((3,)), dma((3,)), dma((3,)), dma((8,)), dma((2, 2)), dma((2, 3)),
            dma((T, 2)), dma((T, 2, 2)), dma((T, 2)), dma((T, 2, 2)), dma((T, 2, 4)), dma((T, 2, 2)),
            dma((T, 2, 2)), dma((T,)),
            dma((T, 2, 4)), dma((T, 2, 2, 4)), dma((T, 2)), dma((T, 2, 2)), dma((T, 2, 2)), dma((T, 2, 2)),
            dma((T, 2, 2)), dma((T,)), dma((T,)), dma((T,)),
        ],
        compiler_params=pltpu.CompilerParams(
            collective_id=0, has_side_effects=True, vmem_limit_bytes=56 << 20
        ),
        name="relay",
    )(
        held[0], arrivals, norm_gain, expert_ids.reshape(T, 4), router_scores.reshape(T, 4),
        w_gate[0], w_up[0], w_down[0],
    )
    return out.reshape(T, 1, 4, D)


def solution(mesh):
    placed = (
        P("section", "expert", None),
        P(None, "expert", None),
        P(None, "section", "expert", None),
        P(None, "section", "expert"),
        P("section", None),
        P("section", None, "expert"),
        P("section", None, "expert"),
        P("section", "expert", None),
    )
    return jax.shard_map(
        per_device,
        mesh=mesh,
        in_specs=placed,
        out_specs=P(None, "section", "expert", None),
        check_vma=False,
    )
```

time: 197 us -> 176 us (0.89)
  the two profiles are of different devices: /device:TPU:193 before, /device:TPU:387 now
where the time goes in v2:
time: 176 us
  Pallas kernels  175 us (99%)
    pallas_call x1, Pallas kernels, per_device(): pl.pallas_call(kernel, out_shape=jax.ShapeDtypeStruct((T, 4, D), BF16), i...  175 us

profile of v2, /device:TPU:387, one launch (start us, length us, event | category | flops | bytes accessed | tf_op | source)
XLA Modules:
  0.0 176.2 jit_solution(17440284602966872905)
XLA Ops:
  0.0 174.5 %relay.1 = bf16[4,4,5120]{2,1,0:T(4,128)(2,1)} custom-call(bf16[4,5120]{1,0:T(4,128)(2,1)} %bitcast.13, bf16[3,4,5120]{2,1,0:T(4,128)(2,1)} %arrivals_ref.1, f32[1,5120]{1,0:T(1,128)} %gain_in.1, s32[4,4]{1,0:T(4,128)} %bitcast.14, f32[4,4]{1,0:T(4,128)} %bitcast.15, bf16[5120,128]{1,0:T(8,128)(2,1)} %bitcast.9, bf16[5120,128]{1,0:T(8,128)(2,1)} %bitcast.10, ...), custom_call_target="tpu_custom_call" | custom-call | tf_op jit(solution)/shard_map/relay/pallas_call | solution.py:368
  174.5 1.6 copy.11

commit v3 on v2

--- a/solution.py
+++ b/solution.py
@@ -19,9 +19,9 @@
 BATCH = ((0, 1), (1, 2), (3, 2), (5, 3))
 BATCH_OF = (0, 1, 1, 2, 2, 3, 3, 3)
 ORDER = (
-    "Asp", "Bd0'", "Bd1'", "Ay1", "Ax0", "Ay2", "Brf'", "Brn'", "Ay3", "Ax1", "Ax2", "Bbf'", "Bbn'", "Ax3",
-    "Ag0", "Ag1", "Bfi'", "Bsp", "Ad0", "Ad1", "By1", "Bx0", "By2", "Arf", "Arn", "By3", "Bx1", "Bx2", "Abf",
-    "Abn", "Bx3", "Bg0", "Bg1", "Afi",
+    "Asp", "Bdn'", "Ay1", "Ax0", "Brf'", "Brn'", "Ay2", "Ay3", "Ax1", "Bbf'", "Bbn'",
+    "Adr'", "Ax2", "Ax3", "Ag0", "Ag1", "Bfi'", "Bsp", "Adn", "By1", "Bx0", "Arf",
+    "Arn", "By2", "By3", "Bx1", "Abf", "Abn", "Bdr'", "Bx2", "Bx3", "Bg0", "Bg1", "Afi",
 )
 F32, BF16 = jnp.float32, jnp.bfloat16
 
@@ -36,12 +36,16 @@
 ):
     section = lax.axis_index("section")
     me = lax.axis_index("expert")
-    core = me % 2
-    py = (me // 2) % NY
-    px = me // (2 * NY)
+    core = lax.rem(me, 2)
+    chip = lax.div(me, 2)
+    py = lax.rem(chip, NY)
+    px = lax.div(chip, NY)
+    chips = {(0, dy): (px * NY + lax.rem(py + dy + NY, NY)) * 2 for dy in DY}
+    chips.update({(dx, 0): (lax.rem(px + dx + NX, NX) * NY + py) * 2 for dx in (1, -1, 2)})
+    above, below = lax.rem(section + 1, 8), lax.rem(section + 7, 8)
 
     def at(dx, dy, c):
-        return {"expert": (((px + dx + NX) % NX) * NY + (py + dy + NY) % NY) * 2 + c}
+        return {"expert": chips[dx, dy] + c}
 
     sibling = at(0, 0, 1 - core)
 
@@ -72,7 +76,7 @@
     partners = [sibling]
     partners += [at(0, dy, c) for dy in DY[1:] for c in range(2)]
     partners += [at(dx, 0, c) for dx in (1, -1) for c in range(2)] + [at(2, 0, core)]
-    partners += [{"section": (section + 1) % 8}, {"section": (section + 7) % 8}]
+    partners += [{"section": above}, {"section": below}]
     for device in partners:
         pl.semaphore_signal(barrier, inc=1, device_id=device, device_id_type=MESH)
 
@@ -188,24 +192,27 @@
         mine_now = pl.ds(low, 64)
         send(exs.at[t, a, mine_now], exr.at[t, a, mine_now], s_ex.at[t, a, s], r_ex.at[t, a, s], sibling)
 
-    def down(t, a, s):
-        low = 64 * s
-        wait(exr.at[t, a, pl.ds(low, 64)], r_ex.at[t, a, s])
-        sums = part[a, low:low + 64] + exr[t, a, low:low + 64].astype(F32)
+    def down(t, a):
+        for s in range(2):
+            wait(exr.at[t, a, pl.ds(64 * s, 64)], r_ex.at[t, a, s])
+        sums = part[a] + exr[t, a].astype(F32)
         gate, up = sums[:, :256], sums[:, 256:]
-        keep = mask[t, a, low:low + 64]
+        keep = mask[t, a]
         hidden = (gate / (1.0 + jnp.exp(-gate)) * up * jnp.concatenate([keep, keep], axis=1)).astype(BF16)
         result = jnp.dot(hidden, wdn[...], preferred_element_type=F32).astype(BF16)
-        piece = jnp.concatenate([result[:, Q * q:Q * q + Q] for q in range(4)], axis=0)
-        moved = jnp.dot(perm_t[...], piece, preferred_element_type=F32).astype(BF16)
-        rs[t, a, 2 * s:2 * s + 2] = moved.reshape(2, 8, 16, Q)
         near, far = pl.ds(0, 4), pl.ds(4, 4)
-        if s:
-            send(rs.at[t, a, 3, far], r1.at[t, a, 1], s_rs.at[t, a, 1], r_r1.at[t, a, 1], at(-1, 0, core))
-            send(rs.at[t, a, 3, near], r1.at[t, a, 0], s_rs.at[t, a, 0], r_r1.at[t, a, 0], at(1, 0, core))
-            send(rs.at[t, a, 2, far], fr.at[t, a, 0, far], s_rs.at[t, a, 2], r_pure.at[t, a, 0], at(1, 0, core))
-        else:
-            send(rs.at[t, a, 1, near], fr.at[t, a, 1, near], s_rs.at[t, a, 3], r_pure.at[t, a, 1], at(-1, 0, core))
+        for s in (1, 0):
+            low = 64 * s
+            piece = jnp.concatenate([result[low:low + 64, Q * q:Q * q + Q] for q in range(4)], axis=0)
+            moved = jnp.dot(perm_t[...], piece, preferred_element_type=F32).astype(BF16)
+            rs[t, a, 2 * s:2 * s + 2] = moved.reshape(2, 8, 16, Q)
+            if s:
+                send(rs.at[t, a, 3, far], r1.at[t, a, 1], s_rs.at[t, a, 1], r_r1.at[t, a, 1], at(-1, 0, core))
+                send(rs.at[t, a, 3, near], r1.at[t, a, 0], s_rs.at[t, a, 0], r_r1.at[t, a, 0], at(1, 0, core))
+                send(rs.at[t, a, 2, far], fr.at[t, a, 0, far], s_rs.at[t, a, 2], r_pure.at[t, a, 0], at(1, 0, core))
+            else:
+                send(rs.at[t, a, 1, near], fr.at[t, a, 1, near], s_rs.at[t, a, 3], r_pure.at[t, a, 1],
+                     at(-1, 0, core))
 
     def relay(t, a, far):
         low = 4 * far
@@ -252,7 +259,7 @@
 
             @pl.when((t < T - 1) & (section < 7))
             def _():
-                send(zsrc.at[t], zbuf.at[t + 1], s_z.at[t], r_z.at[t + 1], {"section": (section + 1) % 8})
+                send(zsrc.at[t], zbuf.at[t + 1], s_z.at[t], r_z.at[t + 1], {"section": above})
 
     def masks():
         for a in range(2):
@@ -264,13 +271,13 @@
 
             send(idb.at[a, 0], idb.at[a, 1], id_send.at[2 + 3 * a], idx_recv.at[a, 0], at(1, 0, core))
             send(idb.at[a, 0], idb.at[a, 2], id_send.at[3 + 3 * a], idx_recv.at[a, 1], at(-1, 0, core))
+
+    def masks_end():
         for a in range(2):
             wait(idb.at[a, 1], idx_recv.at[a, 0])
             wait(idb.at[a, 2], idx_recv.at[a, 1])
             send(idb.at[a, 1], idb.at[a, 3], id_send.at[4 + 3 * a], idx_recv.at[a, 2], at(1, 0, core))
-
-    def masks_end():
-        expert = (px // (NX // 2)).astype(F32)
+        expert = lax.div(px, NX // 2).astype(F32)
         for a in range(2):
             wait(idb.at[a, 3], idx_recv.at[a, 2])
             for g in range(2):
@@ -291,23 +298,47 @@
                 send(ids_ref, idb.at[a, 0, 0], id_send.at[1], id_recv.at[a, 1], sibling)
 
     def ready():
-        masks()
-        masks_end()
         for copy in local:
             copy.wait()
         for k, (_, dst) in enumerate(remote):
             wait(dst, w_recv.at[k])
 
+    def drain(t, a):
+        for d in range(2):
+            wait(ag.at[t, a, 0, pl.ds(1, 7)], s_x.at[t, a, d])
+            wait(fs.at[t, a, d], s_fs.at[t, a, d])
+            wait(exs.at[t, a, pl.ds(64 * d, 64)], s_ex.at[t, a, d])
+        wait(ag.at[t, a, 3], s_x2.at[t, a])
+        for k in range(4):
+            wait(rs.at[t, a, k, pl.ds(0, 4)], s_rs.at[t, a, k])
+        wait(ysrc.at[t, a, pl.ds(1, 7)], s_y.at[t, a, 0])
+
+        @pl.when(core == a)
+        def _():
+            wait(yr.at[t, :, pl.ds(1, 7)], s_own.at[t, 0])
+            wait(yr.at[t, 0, pl.ds(0, 5)], s_own.at[t, 1])
+
+            @pl.when((t < T - 1) & (section < 7))
+            def _():
+                wait(zsrc.at[t], s_z.at[t])
+
+        @pl.when(core != a)
+        def _():
+            wait(ysrc.at[t, a, 0], s_y.at[t, a, 1])
+
     stages = {
+        "dr": drain,
         "sp": spread, "fi": finish,
         "y1": lambda t, a: along_y(t, a, 1), "y2": lambda t, a: along_y(t, a, 2), "y3": lambda t, a: along_y(t, a, 3),
         "x0": lambda t, a: along_x(t, a, 0), "x1": lambda t, a: along_x(t, a, 1),
         "x2": lambda t, a: along_x(t, a, 2), "x3": lambda t, a: along_x(t, a, 3),
         "g0": lambda t, a: gate_up(t, a, 0), "g1": lambda t, a: gate_up(t, a, 1),
-        "d0": lambda t, a: down(t, a, 0), "d1": lambda t, a: down(t, a, 1),
+        "dn": down,
         "rf": lambda t, a: relay(t, a, 1), "rn": lambda t, a: relay(t, a, 0),
         "bf": lambda t, a: back_y(t, a, 1), "bn": lambda t, a: back_y(t, a, 0),
     }
+
+    extra = {"Asp": start, "Ay2": masks, "Ag1": masks_end}
 
     def tick(t, parts, first=False):
         for name in ORDER:
@@ -317,8 +348,8 @@
             if first and name == "Ag0":
                 ready()
             stages[name[1:3]](t - 1 if late else t, "AB".index(name[0]))
-            if first and name == "Asp":
-                start()
+            if first and name in extra:
+                extra[name]()
 
     tick(0, ("now",), first=True)
 
@@ -336,30 +367,6 @@
     for a in range(2):
         for k in range(3):
             wait(idb.at[a, k], id_send.at[2 + 3 * a + k])
-
-    def drain(t, _):
-        wait(yr.at[t, :, pl.ds(1, 7)], s_own.at[t, 0])
-        wait(yr.at[t, 0, pl.ds(0, 5)], s_own.at[t, 1])
-        for a in range(2):
-            for d in range(2):
-                wait(ag.at[t, a, 0, pl.ds(1, 7)], s_x.at[t, a, d])
-                wait(fs.at[t, a, d], s_fs.at[t, a, d])
-                wait(exs.at[t, a, pl.ds(64 * d, 64)], s_ex.at[t, a, d])
-            wait(ag.at[t, a, 3], s_x2.at[t, a])
-            for k in range(4):
-                wait(rs.at[t, a, k, pl.ds(0, 4)], s_rs.at[t, a, k])
-            wait(ysrc.at[t, a, pl.ds(1, 7)], s_y.at[t, a, 0])
-
-            @pl.when(core != a)
-            def _():
-                wait(ysrc.at[t, a, 0], s_y.at[t, a, 1])
-
-        @pl.when((t < T - 1) & (section < 7))
-        def _():
-            wait(zsrc.at[t], s_z.at[t])
-        return 0
-
-    lax.fori_loop(0, T, drain, 0)
 
 
 def per_device(held, arrivals, expert_ids, router_scores, norm_gain, w_gate, w_up, w_down):

time: 176 us -> 169 us (0.960)
  the two profiles are of different devices: /device:TPU:387 before, /device:TPU:257 now
where the time goes in v3:
time: 169 us
  Pallas kernels  168 us (99%)
    pallas_call x1, Pallas kernels, per_device(): pl.pallas_call(kernel, out_shape=jax.ShapeDtypeStruct((T, 4, D), BF16), i...  168 us

profile of v3, /device:TPU:257, one launch (start us, length us, event | category | flops | bytes accessed | tf_op | source)
XLA Modules:
  0.0 169.3 jit_solution(1916659318356380677)
XLA Ops:
  0.0 167.7 %relay.1 = bf16[4,4,5120]{2,1,0:T(4,128)(2,1)} custom-call(bf16[4,5120]{1,0:T(4,128)(2,1)} %bitcast.13, bf16[3,4,5120]{2,1,0:T(4,128)(2,1)} %arrivals_ref.1, f32[1,5120]{1,0:T(1,128)} %gain_in.1, s32[4,4]{1,0:T(4,128)} %bitcast.14, f32[4,4]{1,0:T(4,128)} %bitcast.15, bf16[5120,128]{1,0:T(8,128)(2,1)} %bitcast.9, bf16[5120,128]{1,0:T(8,128)(2,1)} %bitcast.10, ...), custom_call_target="tpu_custom_call" | custom-call | tf_op jit(solution)/shard_map/relay/pallas_call | solution.py:375
  167.7 1.6 copy.11

commit v4 on v3

--- a/solution.py
+++ b/solution.py
@@ -247,19 +247,23 @@
             wait(yr.at[t, 1 - core, 0], r_yc.at[t])
             wait(yr.at[t, :, pl.ds(1, 7)], r_y.at[t])
             weight = score_ref[t]
+            values = []
             for h in range(2):
                 total = yr[t, h, 0].astype(F32)
                 for slot in range(1, 8):
                     total = total + yr[t, h, slot].astype(F32)
-                value = cur[16 * h:16 * h + 16] + weight[16 * h:16 * h + 16, :1] * total
-                zsrc[t, 16 * h:16 * h + 16] = value.astype(BF16)
-                for q in range(4):
-                    k = 4 * h + q
-                    out_ref[t, :, Q * k:Q * k + Q] = value[4 * q:4 * q + 4].astype(BF16)
-
-            @pl.when((t < T - 1) & (section < 7))
-            def _():
-                send(zsrc.at[t], zbuf.at[t + 1], s_z.at[t], r_z.at[t + 1], {"section": above})
+                part_of = pl.ds(16 * h, 16)
+                value = (cur[16 * h:16 * h + 16] + weight[16 * h:16 * h + 16, :1] * total).astype(BF16)
+                zsrc[t, 16 * h:16 * h + 16] = value
+                values.append(value)
+
+                @pl.when((t < T - 1) & (section < 7))
+                def _():
+                    send(zsrc.at[t, part_of], zbuf.at[t + 1, part_of], s_z.at[t], r_z.at[t + 1], {"section": above})
+
+            for k in range(8):
+                row = 4 * (k % 4)
+                out_ref[t, :, Q * k:Q * k + Q] = values[k // 4].astype(F32)[row:row + 4].astype(BF16)
 
     def masks():
         for a in range(2):

time: 169 us -> 170 us (level)
  the two profiles are of different devices: /device:TPU:257 before, /device:TPU:387 now
where the time goes in v4:
time: 170 us; the launch traced here: 169 us
  Pallas kernels  168 us (99%)
    pallas_call x1, Pallas kernels, per_device(): pl.pallas_call(kernel, out_shape=jax.ShapeDtypeStruct((T, 4, D), BF16), i...  168 us

profile of v4, /device:TPU:387, one launch (start us, length us, event | category | flops | bytes accessed | tf_op | source)
XLA Modules:
  0.0 169.5 jit_solution(11468116868381202838)
XLA Ops:
  0.0 167.8 %relay.1 = bf16[4,4,5120]{2,1,0:T(4,128)(2,1)} custom-call(bf16[4,5120]{1,0:T(4,128)(2,1)} %bitcast.13, bf16[3,4,5120]{2,1,0:T(4,128)(2,1)} %arrivals_ref.1, f32[1,5120]{1,0:T(1,128)} %gain_in.1, s32[4,4]{1,0:T(4,128)} %bitcast.14, f32[4,4]{1,0:T(4,128)} %bitcast.15, bf16[5120,128]{1,0:T(8,128)(2,1)} %bitcast.9, bf16[5120,128]{1,0:T(8,128)(2,1)} %bitcast.10, ...), custom_call_target="tpu_custom_call" | custom-call | tf_op jit(solution)/shard_map/relay/pallas_call | solution.py:379
  167.8 1.6 copy.11
